TPU v7x, 512 devices: a whole 4x8x8 slice. The times are simulated.
512 devices in a mesh: clus: 128 (over y, z, core), rep: 4 (over x).
Axes of the slice: x: 4, y: 8, z: 8, core: 2. Of those that a mesh axis runs over, the one named last changes fastest.
Arguments:
- start_vector: bfloat16 [131072, 128], P('clus'), may hold values from -6 to 6
- self_term: float32 [131072], P('clus'), may hold values from 0.5 to 1.5
- near_blocks: bfloat16 [4096, 256, 256], P(('clus', 'rep')), may hold values from -0.09375 to 0.09375
- near_pairs: int32 [4096, 2], P(('clus', 'rep')), may hold values from 0 to 7, as said below
- far_factor: bfloat16 [128, 4, 128, 32, 256], P('clus', 'rep'), may hold values from -0.1875 to 0.1875
- far_cluster: int32 [128, 4, 128], P('clus', 'rep'), may hold values from 0 to 3
Outputs:
- first_image: bfloat16 [131072, 128], P('clus')
- second_image: bfloat16 [131072, 128], P('clus')
Inputs may be any that keep to these rules, and one draw needn't show every extreme that they name: `near_pairs`: column 0 lies in 0 to 3; column 1 is at least column 0 and below 8, and below 4 for pairs of the last slab.
All inputs are finite; a program needn't handle non-finite values.
Results may differ from a plain program's by a relative error of at most 0.01.
Values may be sent and summed in bfloat16 or wider, within the bound.
A program may use at most 64 MiB of HBM per device.

v0:
```python
import jax
import jax.numpy as jnp
from jax import lax
from jax.sharding import PartitionSpec as P


def passed_along(array, axis, by):
    peers = lax.axis_size(axis)
    pairs = [(i, i + by) for i in range(peers) if 0 <= i + by < peers]
    return lax.ppermute(array, axis, pairs)


def apply_operator(vector, near_blocks, near_pairs, zero_filled, self_weight):
    panels, columns = vector.shape
    cluster = near_blocks.shape[1]
    count = panels // cluster
    slab = vector.reshape(count, cluster, columns)
    next_slab = passed_along(slab, "clus", -1)
    extended = jnp.concatenate([slab, next_slab], axis=0)
    row_index = near_pairs[:, 0]
    col_index = near_pairs[:, 1]
    forward = jnp.einsum(
        "pab,pbr->par", near_blocks, extended[col_index], preferred_element_type=jnp.float32
    )
    backward = jnp.einsum(
        "pba,pbr->par", near_blocks, slab[row_index], preferred_element_type=jnp.float32
    )
    positions = jnp.arange(2 * count, dtype=jnp.int32)
    row_table = (row_index[:, None] == positions[None, :]).astype(jnp.float32)
    col_table = (col_index[:, None] == positions[None, :]).astype(jnp.float32)
    near_total = jnp.einsum("pc,par->car", row_table, forward) + jnp.einsum(
        "pc,par->car", col_table, backward
    )
    coefficient = jnp.dot(zero_filled, vector, preferred_element_type=jnp.float32).astype(
        jnp.bfloat16
    )
    partner = lax.all_to_all(coefficient, "clus", split_axis=0, concat_axis=0, tiled=True)
    far_flat = lax.dot_general(
        zero_filled, partner, (((0,), (0,)), ((), ())), preferred_element_type=jnp.float32
    )
    far_total = far_flat.reshape(count, cluster, columns)
    own_part = self_weight.reshape(count, cluster, 1) * slab.astype(jnp.float32)
    own_total = own_part + near_total[:count] + far_total
    next_total = near_total[count:]
    incoming = passed_along(next_total, "clus", 1)
    summed = lax.psum(own_total + incoming, "rep")
    return summed.astype(jnp.bfloat16).reshape(panels, columns)


def local(start_vector, self_term, near_blocks, near_pairs, far_factor, far_cluster):
    cluster = near_blocks.shape[1]
    count = start_vector.shape[0] // cluster
    factors = far_factor.reshape(far_factor.shape[2:])
    owners = far_cluster.reshape(-1)
    ends, rank, width = factors.shape
    owner_table = (owners[:, None] == jnp.arange(count, dtype=jnp.int32)[None, :]).astype(
        jnp.bfloat16
    )
    zero_filled = (owner_table[:, None, :, None] * factors[:, :, None, :]).reshape(
        ends * rank, count * width
    )
    self_weight = jnp.where(lax.axis_index("rep") == 0, self_term, jnp.zeros_like(self_term))
    first_image = apply_operator(start_vector, near_blocks, near_pairs, zero_filled, self_weight)
    second_image = apply_operator(first_image, near_blocks, near_pairs, zero_filled, self_weight)
    return (first_image, second_image)


def solution(mesh):
    placed = (
        P("clus", None),
        P("clus"),
        P(("clus", "rep"), None, None),
        P(("clus", "rep"), None),
        P("clus", "rep", None, None, None),
        P("clus", "rep", None),
    )
    return jax.shard_map(
        local,
        mesh=mesh,
        in_specs=placed,
        out_specs=(P("clus", None), P("clus", None)),
        check_vma=False,
    )
```

profile of v0, /device:TPU:8, one launch (start us, length us, event | category | flops | bytes accessed | tf_op | source)
XLA Modules:
  0.0 190.7 jit_solution(376071644128933086)
XLA Ops:
  0.6 0.8 fusion.10
  1.5 8.8 %broadcast_multiply_fusion = bf16[128,32,4,256]{3,2,1,0:T(4,128)(2,1)} fusion(bf16[128,32,256]{2,1,0:T(8,128)(2,1)} %bitcast.75, bf16[128,4]{1,0:T(8,128)(2,1)S(1)} %fusion.10), kind=kLoop, calls=%fused_computation.6 | loop fusion | flops 4194304 | bytes 10486784 | tf_op jit(solution)/shard_map/mul | solution.py:59
  10.2 9.4 %copy.26 = bf16[512,8,4,256]{3,1,2,0:T(8,128)(2,1)} copy(bf16[512,8,4,256]{3,2,1,0:T(4,128)(2,1)} %bitcast.63) | data formatting | bytes 16777216
  19.7 6.8 %convolution_convert_fusion.1 = bf16[4096,128]{1,0:T(8,128)(2,1)} fusion(bf16[4096,1024]{1,0:T(8,128)(2,1)} %bitcast.64, bf16[1024,128]{1,0:T(8,128)(2,1)S(1)} %copy-done.1), kind=kOutput, calls=%fused_computation.5 | convolution fusion | flops 1074266112 | bytes 9699328 | tf_op jit(solution)/shard_map/dot_general | solution.py:34
  26.4 17.8 %all-to-all-start = ((bf16[128,32,128]{2,1,0:T(8,128)(2,1)}), bf16[128,32,128]{2,1,0:T(8,128)(2,1)}, u32[]{:S(2)}, u32[]{:S(2)}) async-start(bf16[128,32,128]{2,1,0:T(8,128)(2,1)} %bitcast.12), calls=%async_computation | async-start | bytes 2097152 | tf_op jit(solution)/shard_map/all_to_all | solution.py:37
  44.3 4.3 %collective-permute-start = (bf16[4,256,128]{2,1,0:T(8,128)(2,1)S(1)}, bf16[4,256,128]{2,1,0:T(8,128)(2,1)S(1)}, u32[]{:S(2)}, u32[]{:S(2)}) collective-permute-start(bf16[4,256,128]{2,1,0:T(8,128)(2,1)S(1)} %bitcast.69), channel_id=1, source_target_pairs={{4,0},{8,4},{12,8},{16,12},{20,16},{24,20},{28,24},{32,28},{36,32}... | collective-permute-start | bytes 786440 | tf_op jit(solution)/shard_map/ppermute | solution.py:10
  48.8 0.6 gather_fusion.1
  50.2 11.3 %copy.25 = bf16[1024,4096]{1,0:T(8,128)(2,1)} copy(bf16[1024,4096]{0,1:T(8,128)(2,1)} %bitcast.65) | data formatting | bytes 16777216 | tf_op jit(solution)/shard_map/dot_general | solution.py:38
  61.5 9.1 %collective-permute-done = bf16[4,256,128]{2,1,0:T(8,128)(2,1)S(1)} collective-permute-done((bf16[4,256,128]{2,1,0:T(8,128)(2,1)S(1)}, bf16[4,256,128]{2,1,0:T(8,128)(2,1)S(1)}, u32[]{:S(2)}, u32[]{:S(2)}) %collective-permute-start) | collective-permute-done | bytes 262176 | tf_op jit(solution)/shard_map/ppermute | solution.py:10
  70.6 0.6 gather_fusion
  72.8 2.3 %collective-permute-start.1 = (f32[4,256,128]{2,0,1:T(4,128)S(1)}, f32[4,256,128]{2,0,1:T(4,128)S(1)}, u32[]{:S(2)}, u32[]{:S(2)}) collective-permute-start(f32[4,256,128]{2,0,1:T(4,128)S(1)} %slice.35), channel_id=1, source_target_pairs={{0,4},{4,8},{8,12},{12,16},{16,20},{20,24},{24,28},{28,32},{32,36}... | collective-permute-start | bytes 1572872 | tf_op jit(solution)/shard_map/ppermute | solution.py:10
  75.2 5.9 %fusion.25 = f32[4,256,128]{2,1,0:T(8,128)S(1)} fusion(bf16[4,256,4096]{2,1,0:T(8,128)(2,1)} %bitcast.67, bf16[4096,128,1]{1,0,2:T(8,128)(2,1)} %bitcast.14), kind=kOutput, calls=%fused_computation.44 | convolution fusion | flops 1073741824 | bytes 9961472 | tf_op jit(solution)/shard_map/dot_general | solution.py:38
  81.2 4.9 %collective-permute-done.1 = f32[4,256,128]{2,0,1:T(4,128)S(1)} collective-permute-done((f32[4,256,128]{2,0,1:T(4,128)S(1)}, f32[4,256,128]{2,0,1:T(4,128)S(1)}, u32[]{:S(2)}, u32[]{:S(2)}) %collective-permute-start.1) | collective-permute-done | bytes 524320 | tf_op jit(solution)/shard_map/ppermute | solution.py:10
  86.0 0.7 fusion.9
  86.7 22.3 %all-reduce.2 = bf16[4,256,128]{2,0,1:T(4,128)(2,1)S(1)} all-reduce(f32[4,256,128]{2,0,1:T(4,128)S(1)} %fusion.9), channel_id=1, replica_groups=mesh['clus'=128,'rep'=4] {'rep'}, use_global_device_ids=true, to_apply=%region_0.1 | all-reduce | flops 131072 | bytes 786432 | tf_op jit(solution)/shard_map/psum | solution.py:46
  109.1 6.8 %convolution_convert_fusion = bf16[4096,128]{1,0:T(8,128)(2,1)} fusion(bf16[4096,1024]{1,0:T(8,128)(2,1)} %bitcast.66, bf16[1024,128]{1,0:T(8,128)(2,1)S(1)} %bitcast.73), kind=kOutput, calls=%fused_computation.4 | convolution fusion | flops 1074266112 | bytes 9699328 | tf_op jit(solution)/shard_map/dot_general | solution.py:34
  115.9 10.2 %all-to-all-start.1 = ((bf16[128,32,128]{2,1,0:T(8,128)(2,1)}), bf16[128,32,128]{2,1,0:T(8,128)(2,1)}, u32[]{:S(2)}, u32[]{:S(2)}) async-start(bf16[128,32,128]{2,1,0:T(8,128)(2,1)} %bitcast.18), calls=%async_computation.1 | async-start | bytes 2097152 | tf_op jit(solution)/shard_map/all_to_all | solution.py:37
  126.1 4.3 %collective-permute-start.2 = (bf16[4,256,128]{2,0,1:T(4,128)(2,1)S(1)}, bf16[4,256,128]{2,0,1:T(4,128)(2,1)S(1)}, u32[]{:S(2)}, u32[]{:S(2)}) collective-permute-start(bf16[4,256,128]{2,0,1:T(4,128)(2,1)S(1)} %all-reduce.2), channel_id=1, source_target_pairs={{4,0},{8,4},{12,8},{16,12},{20,16},{24,20},{28,24},{32,28},{36,32}... | collective-permute-start | bytes 786440 | tf_op jit(solution)/shard_map/ppermute | solution.py:10
  131.8 20.6 %collective-permute-done.2 = bf16[4,256,128]{2,0,1:T(4,128)(2,1)S(1)} collective-permute-done((bf16[4,256,128]{2,0,1:T(4,128)(2,1)S(1)}, bf16[4,256,128]{2,0,1:T(4,128)(2,1)S(1)}, u32[]{:S(2)}, u32[]{:S(2)}) %collective-permute-start.2) | collective-permute-done | bytes 262176 | tf_op jit(solution)/shard_map/ppermute | solution.py:10
  155.0 2.1 %collective-permute-start.3 = (f32[4,256,128]{2,0,1:T(4,128)S(1)}, f32[4,256,128]{2,0,1:T(4,128)S(1)}, u32[]{:S(2)}, u32[]{:S(2)}) collective-permute-start(f32[4,256,128]{2,0,1:T(4,128)S(1)} %slice.37), channel_id=1, source_target_pairs={{0,4},{4,8},{8,12},{12,16},{16,20},{20,24},{24,28},{28,32},{32,36}... | collective-permute-start | bytes 1572872 | tf_op jit(solution)/shard_map/ppermute | solution.py:10
  157.1 5.9 %fusion.28 = f32[4,256,128]{2,1,0:T(8,128)S(1)} fusion(bf16[4,256,4096]{2,1,0:T(8,128)(2,1)} %bitcast.68, bf16[4096,128,1]{1,0,2:T(8,128)(2,1)} %bitcast.20), kind=kOutput, calls=%fused_computation.47 | convolution fusion | flops 1073741824 | bytes 9961472 | tf_op jit(solution)/shard_map/dot_general | solution.py:38
  163.0 5.2 %collective-permute-done.3 = f32[4,256,128]{2,0,1:T(4,128)S(1)} collective-permute-done((f32[4,256,128]{2,0,1:T(4,128)S(1)}, f32[4,256,128]{2,0,1:T(4,128)S(1)}, u32[]{:S(2)}, u32[]{:S(2)}) %collective-permute-start.3) | collective-permute-done | bytes 524320 | tf_op jit(solution)/shard_map/ppermute | solution.py:10
  168.8 21.1 %all-reduce.3 = bf16[4,256,128]{2,0,1:T(4,128)(2,1)S(1)} all-reduce(f32[4,256,128]{2,0,1:T(4,128)S(1)} %fusion.7), channel_id=1, replica_groups=mesh['clus'=128,'rep'=4] {'rep'}, use_global_device_ids=true, to_apply=%region_1.2 | all-reduce | flops 131072 | bytes 786432 | tf_op jit(solution)/shard_map/psum | solution.py:46
  189.9 0.7 copy.20
  (39 shorter events, 6.9 us)
Async XLA Ops:
  0.6 48.9 %copy-start = (bf16[8,256,256]{2,1,0:T(8,128)(2,1)S(1)}, bf16[8,256,256]{2,1,0:T(8,128)(2,1)}, u32[]{:S(2)}) copy-start(bf16[8,256,256]{2,1,0:T(8,128)(2,1)} %param.8) | copy-start | bytes 3145732
  10.2 9.4 %copy-start.1 = (bf16[1024,128]{1,0:T(8,128)(2,1)S(1)}, bf16[1024,128]{1,0:T(8,128)(2,1)}, u32[]{:S(2)}) copy-start(bf16[1024,128]{1,0:T(8,128)(2,1)} %param.6) | copy-start | bytes 786436
  19.6 29.0 %copy-start.3 = (f32[1024]{0:T(1024)S(1)}, f32[1024]{0:T(1024)}, u32[]{:S(2)}) copy-start(f32[1024]{0:T(1024)} %param.7) | copy-start | bytes 12292
  19.6 29.1 %copy-start.4 = (s32[8,2]{0,1:T(2,128)S(1)}, s32[8,2]{0,1:T(2,128)}, u32[]{:S(2)}) copy-start(s32[8,2]{0,1:T(2,128)} %param.9) | copy-start | bytes 196
  26.4 48.8 %all-to-all-start = ((bf16[128,32,128]{2,1,0:T(8,128)(2,1)}), bf16[128,32,128]{2,1,0:T(8,128)(2,1)}, u32[]{:S(2)}, u32[]{:S(2)}) async-start(bf16[128,32,128]{2,1,0:T(8,128)(2,1)} %bitcast.12), calls=%async_computation | async-start | bytes 2097152 | tf_op jit(solution)/shard_map/all_to_all | solution.py:37
  44.3 26.3 %collective-permute-start = (bf16[4,256,128]{2,1,0:T(8,128)(2,1)S(1)}, bf16[4,256,128]{2,1,0:T(8,128)(2,1)S(1)}, u32[]{:S(2)}, u32[]{:S(2)}) collective-permute-start(bf16[4,256,128]{2,1,0:T(8,128)(2,1)S(1)} %bitcast.69), channel_id=1, source_target_pairs={{4,0},{8,4},{12,8},{16,12},{20,16},{24,20},{28,24},{32,28},{36,32}... | collective-permute-start | bytes 786440 | tf_op jit(solution)/shard_map/ppermute | solution.py:10
  72.8 13.2 %collective-permute-start.1 = (f32[4,256,128]{2,0,1:T(4,128)S(1)}, f32[4,256,128]{2,0,1:T(4,128)S(1)}, u32[]{:S(2)}, u32[]{:S(2)}) collective-permute-start(f32[4,256,128]{2,0,1:T(4,128)S(1)} %slice.35), channel_id=1, source_target_pairs={{0,4},{4,8},{8,12},{12,16},{16,20},{20,24},{24,28},{28,32},{32,36}... | collective-permute-start | bytes 1572872 | tf_op jit(solution)/shard_map/ppermute | solution.py:10
  109.1 22.0 %copy-start.2 = (bf16[4,256,128]{2,1,0:T(8,128)(2,1)}, bf16[4,256,128]{2,1,0:T(8,128)(2,1)S(1)}, u32[]{:S(2)}) copy-start(bf16[4,256,128]{2,1,0:T(8,128)(2,1)S(1)} %copy.15) | copy-start | bytes 786436
  115.9 41.2 %all-to-all-start.1 = ((bf16[128,32,128]{2,1,0:T(8,128)(2,1)}), bf16[128,32,128]{2,1,0:T(8,128)(2,1)}, u32[]{:S(2)}, u32[]{:S(2)}) async-start(bf16[128,32,128]{2,1,0:T(8,128)(2,1)} %bitcast.18), calls=%async_computation.1 | async-start | bytes 2097152 | tf_op jit(solution)/shard_map/all_to_all | solution.py:37
  126.1 26.3 %collective-permute-start.2 = (bf16[4,256,128]{2,0,1:T(4,128)(2,1)S(1)}, bf16[4,256,128]{2,0,1:T(4,128)(2,1)S(1)}, u32[]{:S(2)}, u32[]{:S(2)}) collective-permute-start(bf16[4,256,128]{2,0,1:T(4,128)(2,1)S(1)} %all-reduce.2), channel_id=1, source_target_pairs={{4,0},{8,4},{12,8},{16,12},{20,16},{24,20},{28,24},{32,28},{36,32}... | collective-permute-start | bytes 786440 | tf_op jit(solution)/shard_map/ppermute | solution.py:10
  155.0 13.2 %collective-permute-start.3 = (f32[4,256,128]{2,0,1:T(4,128)S(1)}, f32[4,256,128]{2,0,1:T(4,128)S(1)}, u32[]{:S(2)}, u32[]{:S(2)}) collective-permute-start(f32[4,256,128]{2,0,1:T(4,128)S(1)} %slice.37), channel_id=1, source_target_pairs={{0,4},{4,8},{8,12},{12,16},{16,20},{20,24},{24,28},{28,32},{32,36}... | collective-permute-start | bytes 1572872 | tf_op jit(solution)/shard_map/ppermute | solution.py:10
where the time goes:
time: 192 us; the launch traced here: 191 us
  blocking collectives  43.4 us (23%)
  starting transfers between devices  41.1 us (21%)
  waiting for transfers between devices  39.9 us (21%)
  matrix products  28.2 us (15%)
  local copies, waits for them, and re-layouts  25.8 us (13%)
  other arithmetic  11.2 us (6%)
    psum x2, blocking collectives, apply_operator(): summed = lax.psum(own_total + incoming, 'rep')  43.4 us
    ppermute x4, waiting for transfers between devices, passed_along(): return lax.ppermute(array, axis, pairs)  39.8 us
    all_to_all x2, starting transfers between devices, apply_operator(): lax.all_to_all(coefficient, 'clus', split_axis=0, concat_axis=0, tiled=True)  28.1 us
    dot_general x2, matrix products, apply_operator(): jnp.dot(zero_filled, vector, preferred_element_type=jnp.float32)  13.6 us
    ppermute x4, starting transfers between devices, passed_along(): return lax.ppermute(array, axis, pairs)  13.1 us
    dot_general x2, matrix products, apply_operator(): lax.dot_general(zero_filled, partner, (((0,), (0,)), ((), ())), preferred...  11.9 us
    dot_general x1, local copies, waits for them, and re-layouts, apply_operator(): lax.dot_general(zero_filled, partner, (((0,), (0,)), ((), ())), preferred...  11.3 us
    unnamed x11, local copies, waits for them, and re-layouts  9.44 us
  transfers between devices with their start and end apart: 6, of which 5 were waited for; matrix products, arithmetic and copies ran while one was open for 16% of the time, Pallas kernels for 0%

commit v1 on v0

v1 whole, which is shorter than its diff:
```python
import functools

import jax
import jax.numpy as jnp
from jax import lax
from jax.experimental import pallas as pl
from jax.experimental.pallas import tpu as pltpu
from jax.sharding import PartitionSpec as P

MESH = pl.DeviceIdType.MESH
BF16 = jnp.bfloat16
F32 = jnp.float32

SLABS = 128
REPS = 4
SIDE = 8
CLUSTERS = 4
SIZE = 256
COLS = 128
GROUPS = 2
HALF = COLS // GROUPS
WIDE = CLUSTERS * HALF
QUARTER = SIZE // REPS
RANK = 32
PAIRS = 8
CHUNK = 8


def wrap(value):
    value = jnp.where(value >= SIDE, value - SIDE, value)
    return jnp.where(value < 0, value + SIDE, value)


def to_all_slabs(slab, send):
    core = lax.rem(slab, 2)
    z = lax.rem(slab // 2, SIDE)
    y = slab // (2 * SIDE)

    def to(a, b, other):
        send((wrap(y + a) * SIDE + wrap(z + b)) * 2 + other)

    def four(i, _):
        j = 15 - i // 2
        other = lax.rem(core + i, 2)
        a = 1 + j // 4
        b = lax.rem(j, 4)
        to(a, b, other)
        to(-a, -b, other)
        to(-b, a, other)
        to(b, -a, other)
        return 0

    lax.fori_loop(0, 6, four, 0)
    for other in (0, 1):
        to(4, 0, other)
        to(0, 4, other)
        to(4, 4, other)
    lax.fori_loop(8, 32, four, 0)
    send(slab + 1 - 2 * core)


def swap_halves(x):
    return pltpu.roll(x, HALF, 1)


def kernel(
    pairs, owners, start_in, self_in, near_in, far_in, first_out, second_out,
    start, self_row, near, near_t, far, far_t, vec, self_wide, masks,
    sbuf, rbuf, nextvec, doubled, spread, fwd, bwd, acc, nx_part, nx_got, ns_out, ns_got, xr, result,
    load_sem, out_sem, a2a_s, a2a_r, x_s, x_r, vn_s, vn_r, rl_s, rl_r, nx_s, nx_r, ns_s, ns_r,
):
    slab, rep = lax.axis_index("clus"), lax.axis_index("rep")
    after = jnp.where(slab == SLABS - 1, 0, slab + 1)
    before = jnp.where(slab == 0, SLABS - 1, slab - 1)
    rep_peers = [lax.rem(rep + k, REPS) for k in (2, 1, 3)]

    loads = [
        pltpu.make_async_copy(start_in, start, load_sem.at[0]),
        pltpu.make_async_copy(far_in, far, load_sem.at[1]),
        pltpu.make_async_copy(self_in, self_row, load_sem.at[2]),
    ] + [
        pltpu.make_async_copy(near_in.at[n], near.at[:, pl.ds(n * SIZE, SIZE)], load_sem.at[3 + n])
        for n in range(PAIRS)
    ]
    for load in loads:
        load.start()

    greeting = pltpu.get_barrier_semaphore()

    def greet(peer):
        pl.semaphore_signal(greeting, inc=1, device_id=(peer, rep), device_id_type=MESH)

    to_all_slabs(slab, greet)
    for peer in rep_peers:
        pl.semaphore_signal(greeting, inc=1, device_id=(slab, peer), device_id_type=MESH)

    lane = lax.broadcasted_iota(jnp.int32, (16, COLS), 1)
    low = (lane < HALF).astype(F32).astype(BF16)
    high = (lane >= HALF).astype(F32).astype(BF16)
    block = lax.broadcasted_iota(jnp.int32, (16, 2 * WIDE), 1) // HALF
    for c in range(2 * CLUSTERS):
        masks[c] = (block == c).astype(F32).astype(BF16)

    def merged(x, y):
        rows = x.shape[0]
        x3, y3 = x.reshape(rows // 16, 16, COLS), y.reshape(rows // 16, 16, COLS)
        return (x3 * low[None] + y3 * high[None]).reshape(rows, COLS)

    loads[0].wait()
    for pair in range(CLUSTERS // 2):
        even = start[pl.ds(2 * pair * SIZE, SIZE), :]
        odd = start[pl.ds((2 * pair + 1) * SIZE, SIZE), :]
        part = (REPS, QUARTER, COLS)
        vec[0, 0, :, :, pl.ds(pair * COLS, COLS)] = merged(even, swap_halves(odd)).reshape(part)
        vec[0, 1, :, :, pl.ds(pair * COLS, COLS)] = merged(swap_halves(even), odd).reshape(part)

    def coefficients(m, g):
        values = vec[m, g].reshape(SIZE, WIDE)

        def step(t, _):
            factors = far[pl.ds(t * CHUNK, CHUNK)].reshape(CHUNK * RANK, SIZE)
            full = jnp.dot(factors, values, preferred_element_type=F32).astype(BF16)
            for e in range(CHUNK):
                end = t * CHUNK + e
                mask = masks[owners[end], :, pl.ds(0, WIDE)]
                halves = []
                for top in (0, 16):
                    rows = full[e * RANK + top : e * RANK + top + 16, :] * mask
                    folded = rows[:, :COLS] + rows[:, COLS:]
                    halves.append(folded + swap_halves(folded))
                sbuf[m, g, end] = halves[0] * low + halves[1] * high
            return 0

        lax.fori_loop(0, SLABS // CHUNK, step, 0)
        rbuf[m, g, slab] = sbuf[m, g, slab]

    def send_coefficients(m, g):
        def send(peer):
            pltpu.make_async_remote_copy(
                sbuf.at[m, g, peer], rbuf.at[m, g, slab], a2a_s.at[m, g], a2a_r.at[m, g],
                device_id=(peer, rep), device_id_type=MESH,
            ).start()

        to_all_slabs(slab, send)

    def all_coefficients(m, g):
        others = pl.ds(0, SLABS - 1)
        return pltpu.make_async_remote_copy(
            sbuf.at[m, g, others], rbuf.at[m, g, others], a2a_s.at[m, g], a2a_r.at[m, g],
            device_id=(slab, rep), device_id_type=MESH,
        )

    def next_vector(m, g):
        return pltpu.make_async_remote_copy(
            vec.at[m, g, rep], nextvec.at[m, g, rep], vn_s.at[m, g], vn_r.at[m, g],
            device_id=(before, rep), device_id_type=MESH,
        )

    def relays(m, g):
        return [
            pltpu.make_async_remote_copy(
                nextvec.at[m, g, rep], nextvec.at[m, g, rep], rl_s.at[m, g, k], rl_r.at[m, g, k],
                device_id=(slab, peer), device_id_type=MESH,
            )
            for k, peer in enumerate(rep_peers)
        ]

    def next_parts(m, g):
        return [
            pltpu.make_async_remote_copy(
                nx_part.at[m, g, peer], nx_got.at[m, g, rep], nx_s.at[m, g, k], nx_r.at[m, g, k],
                device_id=(slab, peer), device_id_type=MESH,
            )
            for k, peer in enumerate(rep_peers)
        ]

    def next_sum(m, g):
        return pltpu.make_async_remote_copy(
            ns_out.at[m, g], ns_got.at[m, g], ns_s.at[m, g], ns_r.at[m, g],
            device_id=(after, rep), device_id_type=MESH,
        )

    def exchanges(m, g):
        return [
            pltpu.make_async_remote_copy(
                xr.at[m, g, rep], xr.at[m, g, rep], x_s.at[m, g, k], x_r.at[m, g, k],
                device_id=(slab, peer), device_id_type=MESH,
            )
            for k, peer in enumerate(rep_peers)
        ]

    def near_terms(m, g):
        for base, source in ((0, vec), (CLUSTERS, nextvec)):
            for pair in range(CLUSTERS // 2):
                both = source[m, g, :, :, pl.ds(pair * COLS, COLS)].reshape(SIZE, COLS)
                turned = swap_halves(both)
                doubled[base + 2 * pair] = merged(both, turned)
                doubled[base + 2 * pair + 1] = merged(turned, both)

        def place(n, _):
            a, b = pairs[n, 0], pairs[n, 1]
            tall = (SIZE // 16, 16, COLS)
            column, row = doubled[b].reshape(tall), doubled[a].reshape(tall)
            for k in range(WIDE // COLS):
                mask = masks[a, :, pl.ds(k * COLS, COLS)]
                fwd[n, :, pl.ds(k * COLS, COLS)] = (column * mask[None]).reshape(SIZE, COLS)
            for k in range(2 * WIDE // COLS):
                mask = masks[b, :, pl.ds(k * COLS, COLS)]
                bwd[n, :, pl.ds(k * COLS, COLS)] = (row * mask[None]).reshape(SIZE, COLS)
            return 0

        lax.fori_loop(0, PAIRS, place, 0)
        deep = PAIRS * SIZE
        backward = jnp.dot(near_t[...], bwd[...].reshape(deep, 2 * WIDE), preferred_element_type=F32)
        nx_part[m, g] = backward[:, WIDE:].astype(BF16).reshape(REPS, QUARTER, WIDE)
        acc[m, g] = backward[:, :WIDE]
        acc[m, g] += jnp.dot(near[...], fwd[...].reshape(deep, WIDE), preferred_element_type=F32)
        nx_got[m, g, rep] = nx_part[m, g, rep]
        for copy in next_parts(m, g):
            copy.start()

    def sum_next(m, g):
        for copy in next_parts(m, g):
            copy.wait_recv()
        total = nx_got[m, g, 0].astype(F32)
        for s in range(1, REPS):
            total += nx_got[m, g, s].astype(F32)
        ns_out[m, g] = total.astype(BF16)
        next_sum(m, g).start()

    def far_terms(m, g):
        all_coefficients(m, g).wait_recv()

        def step(t, _):
            for e in range(CHUNK):
                end = t * CHUNK + e
                mask = masks[owners[end], :, pl.ds(0, WIDE)]
                got = rbuf[m, g, end]
                turned = swap_halves(got)
                upper = got * low + turned * high
                lower = turned * low + got * high
                for k in range(WIDE // COLS):
                    part = mask[:, k * COLS : (k + 1) * COLS]
                    lanes = pl.ds(k * COLS, COLS)
                    spread[t, pl.ds(e * RANK, 16), lanes] = upper * part
                    spread[t, pl.ds(e * RANK + 16, 16), lanes] = lower * part
            return 0

        lax.fori_loop(0, SLABS // CHUNK, step, 0)
        total = acc[m, g]
        for q in range(4):
            total += jnp.dot(
                far_t[q], spread[pl.ds(4 * q, 4)].reshape(4 * CHUNK * RANK, WIDE), preferred_element_type=F32
            )
        acc[m, g] = total
        next_sum(m, g).wait_recv()
        mine = pl.ds(pl.multiple_of(rep * QUARTER, QUARTER), QUARTER)
        acc[m, g, mine, :] += ns_got[m, g].astype(F32)
        xr[m, g, rep] = acc[m, g].astype(BF16)
        for copy in exchanges(m, g):
            copy.start()

    def image(m, g):
        for copy in exchanges(m, g):
            copy.wait_recv()
        total = self_wide[...] * vec[m, g].reshape(SIZE, WIDE).astype(F32)
        for s in range(REPS):
            total += xr[m, g, s].astype(F32)
        vec[m + 1, g] = total.astype(BF16).reshape(REPS, QUARTER, WIDE)

    def write(m, out):
        for pair in range(CLUSTERS // 2):
            lanes = pl.ds(pair * COLS, COLS)
            a = vec[m + 1, 0, :, :, lanes].reshape(SIZE, COLS)
            b = vec[m + 1, 1, :, :, lanes].reshape(SIZE, COLS)
            result[m, pl.ds(2 * pair * SIZE, SIZE), :] = merged(a, swap_halves(b))
            result[m, pl.ds((2 * pair + 1) * SIZE, SIZE), :] = merged(swap_halves(a), b)
        pltpu.make_async_copy(result.at[m], out, out_sem.at[m]).start()

    loads[1].wait()
    coefficients(0, 0)
    pl.semaphore_wait(greeting, SLABS - 1 + REPS - 1)
    next_vector(0, 0).start()
    next_vector(0, 1).start()
    send_coefficients(0, 0)
    coefficients(0, 1)
    send_coefficients(0, 1)

    for load in loads[2:]:
        load.wait()
    for n in range(PAIRS):
        near_t[:, pl.ds(n * SIZE, SIZE)] = near[:, pl.ds(n * SIZE, SIZE)].T
    for t in range(SLABS // CHUNK):
        tile = far[pl.ds(t * CHUNK, CHUNK)].reshape(CHUNK * RANK, SIZE)
        far_t[t // 4, :, pl.ds((t % 4) * CHUNK * RANK, CHUNK * RANK)] = tile.T
    wide = [
        jnp.broadcast_to(
            jnp.concatenate([self_row[2 * c : 2 * c + 1, :], self_row[2 * c + 1 : 2 * c + 2, :]], axis=1),
            (HALF, SIZE),
        )
        for c in range(CLUSTERS)
    ]
    self_wide[...] = jnp.concatenate(wide, axis=0).T

    def pass_on(m, g):
        next_vector(m, g).wait_recv()
        for copy in relays(m, g):
            copy.start()

    def near_part(m, g):
        for copy in relays(m, g):
            copy.wait_recv()
        near_terms(m, g)

    pass_on(0, 0)
    pass_on(0, 1)
    near_part(0, 0)
    near_part(0, 1)
    sum_next(0, 0)
    sum_next(0, 1)
    far_terms(0, 0)
    image(0, 0)
    next_vector(1, 0).start()
    coefficients(1, 0)
    send_coefficients(1, 0)
    far_terms(0, 1)
    pass_on(1, 0)
    image(0, 1)
    next_vector(1, 1).start()
    coefficients(1, 1)
    send_coefficients(1, 1)
    write(0, first_out)
    pass_on(1, 1)
    near_part(1, 0)
    near_part(1, 1)
    sum_next(1, 0)
    sum_next(1, 1)
    far_terms(1, 0)
    image(1, 0)
    far_terms(1, 1)
    image(1, 1)
    write(1, second_out)

    for m in range(2):
        for g in range(GROUPS):
            all_coefficients(m, g).wait_send()
            next_vector(m, g).wait_send()
            next_sum(m, g).wait_send()
            for copy in relays(m, g) + next_parts(m, g) + exchanges(m, g):
                copy.wait_send()
    pltpu.make_async_copy(result.at[0], first_out, out_sem.at[0]).wait()
    pltpu.make_async_copy(result.at[1], second_out, out_sem.at[1]).wait()


def local(start_vector, self_term, near_blocks, near_pairs, far_factor, far_cluster):
    panels, columns = start_vector.shape
    factors = far_factor.reshape(far_factor.shape[2:])
    owners = far_cluster.reshape(-1)
    self_rows = self_term.reshape(panels // COLS, COLS)
    vmem, dma = pltpu.VMEM, pltpu.SemaphoreType.DMA
    image = jax.ShapeDtypeStruct((panels, columns), BF16)
    both = (2, GROUPS)
    scratch = [
        vmem((panels, columns), BF16),
        vmem(self_rows.shape, F32),
        vmem((SIZE, PAIRS * SIZE), BF16),
        vmem((SIZE, PAIRS * SIZE), BF16),
        vmem(factors.shape, BF16),
        vmem((4, SIZE, SLABS // 4 * RANK), BF16),
        vmem((3, GROUPS, REPS, QUARTER, WIDE), BF16),
        vmem((SIZE, WIDE), F32),
        vmem((2 * CLUSTERS, 16, 2 * WIDE), BF16),
        vmem(both + (SLABS, 16, COLS), BF16),
        vmem(both + (SLABS, 16, COLS), BF16),
        vmem(both + (REPS, QUARTER, WIDE), BF16),
        vmem((2 * CLUSTERS, SIZE, COLS), BF16),
        vmem((SLABS // CHUNK, CHUNK * RANK, WIDE), BF16),
        vmem((PAIRS, SIZE, WIDE), BF16),
        vmem((PAIRS, SIZE, 2 * WIDE), BF16),
        vmem(both + (SIZE, WIDE), F32),
        vmem(both + (REPS, QUARTER, WIDE), BF16),
        vmem(both + (REPS, QUARTER, WIDE), BF16),
        vmem(both + (QUARTER, WIDE), BF16),
        vmem(both + (QUARTER, WIDE), BF16),
        vmem(both + (REPS, SIZE, WIDE), BF16),
        vmem((2, panels, columns), BF16),
        dma((3 + PAIRS,)),
        dma((2,)),
        dma(both), dma(both),
        dma(both + (3,)), dma(both + (3,)),
        dma(both), dma(both),
        dma(both + (3,)), dma(both + (3,)),
        dma(both + (3,)), dma(both + (3,)),
        dma(both), dma(both),
    ]
    smem = pl.BlockSpec(memory_space=pltpu.SMEM)
    hbm = pl.BlockSpec(memory_space=pl.ANY)
    return pl.pallas_call(
        kernel,
        out_shape=(image, image),
        in_specs=[smem, smem, hbm, hbm, hbm, hbm],
        out_specs=(hbm, hbm),
        scratch_shapes=scratch,
        compiler_params=pltpu.CompilerParams(
            collective_id=0, has_side_effects=True, vmem_limit_bytes=52 * 1024 * 1024
        ),
        name="two_products",
    )(near_pairs, owners, start_vector, self_rows, near_blocks, factors)


def solution(mesh):
    placed = (
        P("clus", None),
        P("clus"),
        P(("clus", "rep"), None, None),
        P(("clus", "rep"), None),
        P("clus", "rep", None, None, None),
        P("clus", "rep", None),
    )
    return jax.shard_map(
        local,
        mesh=mesh,
        in_specs=placed,
        out_specs=(P("clus", None), P("clus", None)),
        check_vma=False,
    )
```

time: 192 us -> 115 us (0.60)
  the two profiles are of different devices: /device:TPU:8 before, /device:TPU:2 now
where the time goes in v1:
time: 115 us; the launch traced here: 114 us
  Pallas kernels  108 us (94%)
  local copies, waits for them, and re-layouts  5.68 us (5%)
    pallas_call x1, Pallas kernels, local(): pl.pallas_call(kernel, out_shape=(image, image), in_specs=[smem, smem, hb...  108 us
    unnamed x11, local copies, waits for them, and re-layouts  5.68 us

profile of v1, /device:TPU:2, one launch (start us, length us, event | category | flops | bytes accessed | tf_op | source)
XLA Modules:
  0.0 114.4 jit_solution(8065812507358624355)
XLA Ops:
  0.6 0.8 copy.8.pairs
  1.4 0.0 copy-start
  1.4 1.2 %copy-done = bf16[8,256,256]{2,1,0:T(8,128)(2,1)S(1)} copy-done((bf16[8,256,256]{2,1,0:T(8,128)(2,1)S(1)}, bf16[8,256,256]{2,1,0:T(8,128)(2,1)}, u32[]{:S(2)}) %copy-start) | copy-done | bytes 1048600
  2.6 0.0 copy-start.1
  2.6 0.9 copy-done.1
  3.6 0.0 copy-start.2
  3.6 0.7 copy-done.2
  4.2 0.0 copy-start.3
  4.2 0.7 copy-done.3
  4.9 108.1 %two_products.1 = (bf16[1024,128]{1,0:T(8,128)(2,1)S(1)}, bf16[1024,128]{1,0:T(8,128)(2,1)S(1)}) custom-call(s32[8,2]{1,0:T(8,128)S(1)} %copy.8.pairs, s32[128]{0:T(128)S(1)} %bitcast.4, bf16[1024,128]{1,0:T(8,128)(2,1)S(1)} %copy-done.1, f32[8,128]{1,0:T(8,128)S(1)} %bitcast.3, bf16[8,256,256]{2,1,0:T(8,128)(2,1)S(1)} %copy-done, bf16[128,32,256]{2,1,0:T(8,128)(2,1)} %bitcast.5), custom_call_target="tpu_custom_call" | custom-call | tf_op jit(solution)/shard_map/two_products/pallas_call | solution.py:398
  113.0 0.7 copy.11
  113.7 0.7 copy.12
Async XLA Ops:
  1.4 1.2 %copy-start = (bf16[8,256,256]{2,1,0:T(8,128)(2,1)S(1)}, bf16[8,256,256]{2,1,0:T(8,128)(2,1)}, u32[]{:S(2)}) copy-start(bf16[8,256,256]{2,1,0:T(8,128)(2,1)} %near_in.1) | copy-start | bytes 3145732
  2.6 0.9 copy-start.1
  3.6 0.7 copy-start.2
  4.2 0.7 copy-start.3

commit v2 on v1

v2 whole, which is shorter than its diff:
```python
import functools

import jax
import jax.numpy as jnp
from jax import lax
from jax.experimental import pallas as pl
from jax.experimental.pallas import tpu as pltpu
from jax.sharding import PartitionSpec as P

MESH = pl.DeviceIdType.MESH
BF16 = jnp.bfloat16
F32 = jnp.float32

SLABS = 128
REPS = 4
SIDE = 8
CLUSTERS = 4
SIZE = 256
COLS = 128
GROUPS = 2
HALF = COLS // GROUPS
WIDE = CLUSTERS * HALF
QUARTER = SIZE // REPS
RANK = 32
PAIRS = 8
CHUNK = 8
SETS = SLABS // CHUNK
SELF_SET = 3
STEP = 4
STAGES = SETS // STEP


def wrap(value):
    value = jnp.where(value >= SIDE, value - SIDE, value)
    return jnp.where(value < 0, value + SIDE, value)


def ring(slab, i):
    core = lax.rem(slab, 2)
    z = lax.rem(slab // 2, SIDE)
    y = slab // (2 * SIDE)
    j = 15 - i
    a, b = 1 + j // 4, j % 4
    turns = [(a, b), (-a, -b), (-b, a), (b, -a)]
    if isinstance(i, int):
        if i == SELF_SET:
            turns = [(4, 0), (4, 4), (0, 4), (0, 0)]
    else:
        odd = i == SELF_SET
        turns[1] = (jnp.where(odd, 4, -a), jnp.where(odd, 4, -b))
        turns[3] = (jnp.where(odd, 0, b), jnp.where(odd, 0, -a))
    places = [(wrap(y + p) * SIDE + wrap(z + q)) * 2 for p, q in turns]
    return [p + 1 - core for p in places] + [p + core for p in places]


def swap_halves(x):
    return pltpu.roll(x, HALF, 1)


def kernel(
    pairs_in, owners_in, start_in, self_in, near_in, far_in, first, second,
    pairs, owners,
    start, self_row, near, near_t, far, far_t, vec, self_wide, masks,
    sbuf, rbuf, nextvec, doubled, fwd, bwd, acc, nx_part, nx_got, ns_out, ns_got, xr,
    load_sem, out_sem, a2a_s, a2a_r, x_s, x_r, vn_s, vn_r, rl_s, rl_r, nx_s, nx_r, ns_s, ns_r,
):
    slab, rep = lax.axis_index("clus"), lax.axis_index("rep")
    after = jnp.where(slab == SLABS - 1, 0, slab + 1)
    before = jnp.where(slab == 0, SLABS - 1, slab - 1)
    rep_peers = [lax.rem(rep + k, REPS) for k in (2, 1, 3)]

    loads = [
        pltpu.make_async_copy(start_in, start, load_sem.at[0]),
        pltpu.make_async_copy(far_in, far, load_sem.at[1]),
        pltpu.make_async_copy(owners_in, owners, load_sem.at[2]),
        pltpu.make_async_copy(self_in, self_row, load_sem.at[3]),
        pltpu.make_async_copy(pairs_in, pairs, load_sem.at[4]),
    ] + [
        pltpu.make_async_copy(near_in.at[n], near.at[:, pl.ds(n * SIZE, SIZE)], load_sem.at[5 + n])
        for n in range(PAIRS)
    ]
    for load in loads:
        load.start()

    greeting = pltpu.get_barrier_semaphore()

    def greet(peer):
        pl.semaphore_signal(greeting, inc=1, device_id=(peer, rep), device_id_type=MESH)

    for i in range(SETS):
        for e, peer in enumerate(ring(slab, i)):
            if (i, e) != (SELF_SET, CHUNK - 1):
                greet(peer)
    for peer in rep_peers:
        pl.semaphore_signal(greeting, inc=1, device_id=(slab, peer), device_id_type=MESH)

    lane = lax.broadcasted_iota(jnp.int32, (16, COLS), 1)
    low = (lane < HALF).astype(F32).astype(BF16)
    high = (lane >= HALF).astype(F32).astype(BF16)
    block = lax.broadcasted_iota(jnp.int32, (16, 2 * WIDE), 1) // HALF
    for c in range(2 * CLUSTERS):
        masks[c] = (block == c).astype(F32).astype(BF16)

    def merged(x, y):
        rows = x.shape[0]
        x3, y3 = x.reshape(rows // 16, 16, COLS), y.reshape(rows // 16, 16, COLS)
        return (x3 * low[None] + y3 * high[None]).reshape(rows, COLS)

    loads[0].wait()
    for pair in range(CLUSTERS // 2):
        even = start[pl.ds(2 * pair * SIZE, SIZE), :]
        odd = start[pl.ds((2 * pair + 1) * SIZE, SIZE), :]
        part = (REPS, QUARTER, COLS)
        vec[0, 0, :, :, pl.ds(pair * COLS, COLS)] = merged(even, swap_halves(odd)).reshape(part)
        vec[0, 1, :, :, pl.ds(pair * COLS, COLS)] = merged(swap_halves(even), odd).reshape(part)

    def coefficients(m, g, first=0, last=STAGES):
        values = vec[m, g].reshape(SIZE, WIDE)

        def multiply(ends):
            factors = jnp.concatenate([far[end] for end in ends], axis=0)
            return jnp.dot(factors, values, preferred_element_type=F32).astype(BF16)

        def pick(full, ends):
            for e, end in enumerate(ends):
                mask = masks[owners[end], :, pl.ds(0, WIDE)]
                halves = []
                for top in (0, 16):
                    rows = full[e * RANK + top : e * RANK + top + 16, :] * mask
                    folded = rows[:, :COLS] + rows[:, COLS:]
                    halves.append(folded + swap_halves(folded))
                sbuf[m, g, end] = halves[0] * low + halves[1] * high

        def send(stage, k, e, end):
            copy = pltpu.make_async_remote_copy(
                sbuf.at[m, g, end], rbuf.at[m, g, slab], a2a_s.at[m, g], a2a_r.at[m, g, stage],
                device_id=(end, rep), device_id_type=MESH,
            )
            if k == SELF_SET and e == CHUNK - 1:
                pl.when(stage > 0)(copy.start)
            else:
                copy.start()

        def step(stage, _):
            sets = [ring(slab, stage * STEP + k) for k in range(STEP)]
            full = [multiply(ends) for ends in sets]
            for k, ends in enumerate(sets):
                pick(full[k], ends)
            for k, ends in enumerate(sets):
                for e, end in enumerate(ends):
                    send(stage, k, e, end)
            return 0

        lax.fori_loop(first, last, step, 0)
        if first == 0:
            rbuf[m, g, slab] = sbuf[m, g, slab]

    def sent(m, g):
        others = pl.ds(0, SLABS - 1)
        return pltpu.make_async_remote_copy(
            sbuf.at[m, g, others], rbuf.at[m, g, others], a2a_s.at[m, g], a2a_r.at[m, g, 0],
            device_id=(slab, rep), device_id_type=MESH,
        )

    def received(m, g, stage, count):
        some = pl.ds(0, count)
        return pltpu.make_async_remote_copy(
            sbuf.at[m, g, some], rbuf.at[m, g, some], a2a_s.at[m, g], a2a_r.at[m, g, stage],
            device_id=(slab, rep), device_id_type=MESH,
        )

    def next_vector(m, g):
        return pltpu.make_async_remote_copy(
            vec.at[m, g, rep], nextvec.at[m, g, rep], vn_s.at[m, g], vn_r.at[m, g],
            device_id=(before, rep), device_id_type=MESH,
        )

    def relays(m, g):
        return [
            pltpu.make_async_remote_copy(
                nextvec.at[m, g, rep], nextvec.at[m, g, rep], rl_s.at[m, g, k], rl_r.at[m, g, k],
                device_id=(slab, peer), device_id_type=MESH,
            )
            for k, peer in enumerate(rep_peers)
        ]

    def next_parts(m, g):
        return [
            pltpu.make_async_remote_copy(
                nx_part.at[m, g, peer], nx_got.at[m, g, rep], nx_s.at[m, g, k], nx_r.at[m, g, k],
                device_id=(slab, peer), device_id_type=MESH,
            )
            for k, peer in enumerate(rep_peers)
        ]

    def next_sum(m, g):
        return pltpu.make_async_remote_copy(
            ns_out.at[m, g], ns_got.at[m, g], ns_s.at[m, g], ns_r.at[m, g],
            device_id=(after, rep), device_id_type=MESH,
        )

    def exchanges(m, g):
        return [
            pltpu.make_async_remote_copy(
                xr.at[m, g, rep], xr.at[m, g, rep], x_s.at[m, g, k], x_r.at[m, g, k],
                device_id=(slab, peer), device_id_type=MESH,
            )
            for k, peer in enumerate(rep_peers)
        ]

    def double(m, g, source, base):
        for pair in range(CLUSTERS // 2):
            both = source[m, g, :, :, pl.ds(pair * COLS, COLS)].reshape(SIZE, COLS)
            turned = swap_halves(both)
            doubled[g, base + 2 * pair] = merged(both, turned)
            doubled[g, base + 2 * pair + 1] = merged(turned, both)

    def backward(m, g):
        double(m, g, vec, 0)

        def place(n, _):
            a, b = pairs[0, n], pairs[1, n]
            values = doubled[g, a].reshape(SIZE // 16, 16, COLS)
            for k in range(2 * WIDE // COLS):
                mask = masks[b, :, pl.ds(k * COLS, COLS)]
                bwd[n, :, pl.ds(k * COLS, COLS)] = (values * mask[None]).reshape(SIZE, COLS)
            return 0

        lax.fori_loop(0, PAIRS, place, 0)
        terms = jnp.dot(near_t[...], bwd[...].reshape(PAIRS * SIZE, 2 * WIDE), preferred_element_type=F32)
        nx_part[m, g] = terms[:, WIDE:].astype(BF16).reshape(REPS, QUARTER, WIDE)
        acc[m, g] = terms[:, :WIDE]
        nx_got[m, g, rep] = nx_part[m, g, rep]
        for copy in next_parts(m, g):
            copy.start()

    def forward(m, g):
        for copy in relays(m, g):
            copy.wait_recv()
        double(m, g, nextvec, CLUSTERS)

        def place(n, _):
            a, b = pairs[0, n], pairs[1, n]
            values = doubled[g, b].reshape(SIZE // 16, 16, COLS)
            for k in range(WIDE // COLS):
                mask = masks[a, :, pl.ds(k * COLS, COLS)]
                fwd[n, :, pl.ds(k * COLS, COLS)] = (values * mask[None]).reshape(SIZE, COLS)
            return 0

        lax.fori_loop(0, PAIRS, place, 0)
        acc[m, g] += jnp.dot(near[...], fwd[...].reshape(PAIRS * SIZE, WIDE), preferred_element_type=F32)

    def sum_next(m, g):
        for copy in next_parts(m, g):
            copy.wait_recv()
        total = nx_got[m, g, 0].astype(F32)
        for s in range(1, REPS):
            total += nx_got[m, g, s].astype(F32)
        ns_out[m, g] = total.astype(BF16)
        next_sum(m, g).start()

    def far_terms(m, g):
        def step(stage, _):
            if isinstance(stage, int):
                received(m, g, stage, STEP * CHUNK - 1).wait_recv()
            else:
                received(m, g, stage, STEP * CHUNK).wait_recv()
            tiles = []
            for k in range(STEP):
                for end in ring(slab, stage * STEP + k):
                    mask = masks[owners[end], :, pl.ds(0, WIDE)]
                    got = rbuf[m, g, end]
                    turned = swap_halves(got)
                    for part in (got * low + turned * high, turned * low + got * high):
                        tiles.append(jnp.concatenate([part] * (WIDE // COLS), axis=1) * mask)
            spread = jnp.concatenate(tiles, axis=0)
            acc[m, g] += jnp.dot(far_t[stage], spread, preferred_element_type=F32)
            return 0

        step(0, 0)
        lax.fori_loop(1, STAGES, step, 0)
        next_sum(m, g).wait_recv()
        mine = pl.ds(pl.multiple_of(rep * QUARTER, QUARTER), QUARTER)
        acc[m, g, mine, :] += ns_got[m, g].astype(F32)
        xr[m, g, rep] = acc[m, g].astype(BF16)
        for copy in exchanges(m, g):
            copy.start()

    def image(m, g):
        for copy in exchanges(m, g):
            copy.wait_recv()
        total = self_wide[...] * vec[m, g].reshape(SIZE, WIDE).astype(F32)
        for s in range(REPS):
            total += xr[m, g, s].astype(F32)
        vec[m + 1, g] = total.astype(BF16).reshape(REPS, QUARTER, WIDE)

    def write(m, out):
        return pltpu.make_async_copy(vec.at[m + 1], out, out_sem.at[m])

    loads[1].wait()
    loads[2].wait()
    pl.semaphore_wait(greeting, SLABS - 1 + REPS - 1)
    next_vector(0, 0).start()
    next_vector(0, 1).start()
    coefficients(0, 0)

    for load in loads[3:]:
        load.wait()
    for n in range(PAIRS):
        near_t[:, pl.ds(n * SIZE, SIZE)] = near[:, pl.ds(n * SIZE, SIZE)].T
    backward(0, 0)
    backward(0, 1)

    def pass_on(m, g):
        next_vector(m, g).wait_recv()
        for copy in relays(m, g):
            copy.start()

    pass_on(0, 0)
    pass_on(0, 1)
    coefficients(0, 1)
    sum_next(0, 0)
    sum_next(0, 1)
    forward(0, 0)

    for i in range(SETS):
        tile = jnp.concatenate([far[end] for end in ring(slab, i)], axis=0)
        far_t[i // STEP, :, pl.ds((i % STEP) * CHUNK * RANK, CHUNK * RANK)] = tile.T
    wide = [
        jnp.broadcast_to(
            jnp.concatenate([self_row[2 * c : 2 * c + 1, :], self_row[2 * c + 1 : 2 * c + 2, :]], axis=1),
            (HALF, SIZE),
        )
        for c in range(CLUSTERS)
    ]
    self_wide[...] = jnp.concatenate(wide, axis=0).T

    far_terms(0, 0)
    image(0, 0)
    next_vector(1, 0).start()
    coefficients(1, 0)
    forward(0, 1)
    far_terms(0, 1)
    backward(1, 0)
    pass_on(1, 0)
    sum_next(1, 0)
    image(0, 1)
    next_vector(1, 1).start()
    coefficients(1, 1)
    forward(1, 0)
    backward(1, 1)
    far_terms(1, 0)
    pass_on(1, 1)
    sum_next(1, 1)
    write(0, first).start()
    forward(1, 1)
    image(1, 0)
    far_terms(1, 1)
    image(1, 1)
    write(1, second).start()

    for m in range(2):
        for g in range(GROUPS):
            sent(m, g).wait_send()
            next_vector(m, g).wait_send()
            next_sum(m, g).wait_send()
            for copy in relays(m, g) + next_parts(m, g) + exchanges(m, g):
                copy.wait_send()
    write(0, first).wait()
    write(1, second).wait()


def lay_out(first, second, first_out, second_out):
    lane = lax.broadcasted_iota(jnp.int32, (SIZE, COLS), 1)
    for source, out in ((first, first_out), (second, second_out)):
        for pair in range(CLUSTERS // 2):
            lanes = pl.ds(pair * COLS, COLS)
            a = source[0, :, :, lanes].reshape(SIZE, COLS)
            b = source[1, :, :, lanes].reshape(SIZE, COLS)
            out[pl.ds(2 * pair * SIZE, SIZE), :] = jnp.where(lane < HALF, a, swap_halves(b))
            out[pl.ds((2 * pair + 1) * SIZE, SIZE), :] = jnp.where(lane < HALF, swap_halves(a), b)


def local(start_vector, self_term, near_blocks, near_pairs, far_factor, far_cluster):
    panels, columns = start_vector.shape
    factors = far_factor.reshape(far_factor.shape[2:])
    owners = far_cluster.reshape(-1)
    pairs = near_pairs.T
    self_rows = self_term.reshape(panels // COLS, COLS)
    vmem, dma = pltpu.VMEM, pltpu.SemaphoreType.DMA
    image = jax.ShapeDtypeStruct((panels, columns), BF16)
    grouped = jax.ShapeDtypeStruct((GROUPS, REPS, QUARTER, WIDE), BF16)
    both = (2, GROUPS)
    scratch = [
        pltpu.SMEM(pairs.shape, jnp.int32),
        pltpu.SMEM(owners.shape, jnp.int32),
        vmem((panels, columns), BF16),
        vmem(self_rows.shape, F32),
        vmem((SIZE, PAIRS * SIZE), BF16),
        vmem((SIZE, PAIRS * SIZE), BF16),
        vmem(factors.shape, BF16),
        vmem((STAGES, SIZE, STEP * CHUNK * RANK), BF16),
        vmem((3, GROUPS, REPS, QUARTER, WIDE), BF16),
        vmem((SIZE, WIDE), F32),
        vmem((2 * CLUSTERS, 16, 2 * WIDE), BF16),
        vmem(both + (SLABS, 16, COLS), BF16),
        vmem(both + (SLABS, 16, COLS), BF16),
        vmem(both + (REPS, QUARTER, WIDE), BF16),
        vmem((GROUPS, 2 * CLUSTERS, SIZE, COLS), BF16),
        vmem((PAIRS, SIZE, WIDE), BF16),
        vmem((PAIRS, SIZE, 2 * WIDE), BF16),
        vmem(both + (SIZE, WIDE), F32),
        vmem(both + (REPS, QUARTER, WIDE), BF16),
        vmem(both + (REPS, QUARTER, WIDE), BF16),
        vmem(both + (QUARTER, WIDE), BF16),
        vmem(both + (QUARTER, WIDE), BF16),
        vmem(both + (REPS, SIZE, WIDE), BF16),
        dma((5 + PAIRS,)),
        dma((2,)),
        dma(both), dma(both + (STAGES,)),
        dma(both + (3,)), dma(both + (3,)),
        dma(both), dma(both),
        dma(both + (3,)), dma(both + (3,)),
        dma(both + (3,)), dma(both + (3,)),
        dma(both), dma(both),
    ]
    hbm = pl.BlockSpec(memory_space=pl.ANY)
    whole = pl.BlockSpec(memory_space=pltpu.VMEM)
    images = pl.pallas_call(
        kernel,
        out_shape=(grouped, grouped),
        in_specs=[hbm] * 6,
        out_specs=(hbm, hbm),
        scratch_shapes=scratch,
        compiler_params=pltpu.CompilerParams(
            collective_id=0, has_side_effects=True, vmem_limit_bytes=60 * 1024 * 1024
        ),
        name="two_products",
    )(pairs, owners, start_vector, self_rows, near_blocks, factors)
    return pl.pallas_call(
        lay_out,
        out_shape=(image, image),
        in_specs=[whole, whole],
        out_specs=(whole, whole),
        name="lay_out",
    )(*images)


def solution(mesh):
    placed = (
        P("clus", None),
        P("clus"),
        P(("clus", "rep"), None, None),
        P(("clus", "rep"), None),
        P("clus", "rep", None, None, None),
        P("clus", "rep", None),
    )
    return jax.shard_map(
        local,
        mesh=mesh,
        in_specs=placed,
        out_specs=(P("clus", None), P("clus", None)),
        check_vma=False,
    )
```

time: 115 us -> 91 us (0.79)
  the two profiles are of different devices: /device:TPU:2 before, /device:TPU:64 now
where the time goes in v2:
time: 91 us; the launch traced here: 90.8 us
  Pallas kernels  90.2 us (99%)
    pallas_call x1, Pallas kernels, local(): pl.pallas_call(kernel, out_shape=(grouped, grouped), in_specs=[hbm] * 6,...  88.2 us
    pallas_call x1, Pallas kernels, local(): pl.pallas_call(lay_out, out_shape=(image, image), in_specs=[whole, whole]...  1.96 us

profile of v2, /device:TPU:64, one launch (start us, length us, event | category | flops | bytes accessed | tf_op | source)
XLA Modules:
  0.0 90.8 jit_solution(12797401116986641891)
XLA Ops:
  0.6 88.2 %two_products.1 = (bf16[2,4,64,256]{3,2,1,0:T(8,128)(2,1)}, bf16[2,4,64,256]{3,2,1,0:T(8,128)(2,1)}) custom-call(s32[2,8]{1,0:T(2,128)} %bitcast.6, s32[128]{0:T(128)} %bitcast.7, bf16[1024,128]{1,0:T(8,128)(2,1)} %start_in.1, f32[8,128]{1,0:T(8,128)} %bitcast.5, bf16[8,256,256]{2,1,0:T(8,128)(2,1)} %near_in.1, bf16[128,32,256]{2,1,0:T(8,128)(2,1)} %bitcast.4), custom_call_target="tpu_custom_call" | custom-call | tf_op jit(solution)/shard_map/two_products/pallas_call | solution.py:429
  88.9 2.0 %lay_out.1 = (bf16[1024,128]{1,0:T(8,128)(2,1)}, bf16[1024,128]{1,0:T(8,128)(2,1)}) custom-call(bf16[2,4,64,256]{3,2,1,0:T(8,128)(2,1)} %get-tuple-element.4.first, bf16[2,4,64,256]{3,2,1,0:T(8,128)(2,1)} %get-tuple-element.5.second), custom_call_target="tpu_custom_call" | custom-call | tf_op jit(solution)/shard_map/lay_out/pallas_call | solution.py:440

commit v3 on v2

--- a/solution.py
+++ b/solution.py
@@ -61,8 +61,8 @@
     pairs_in, owners_in, start_in, self_in, near_in, far_in, first, second,
     pairs, owners,
     start, self_row, near, near_t, far, far_t, vec, self_wide, masks,
-    sbuf, rbuf, nextvec, doubled, fwd, bwd, acc, nx_part, nx_got, ns_out, ns_got, xr,
-    load_sem, out_sem, a2a_s, a2a_r, x_s, x_r, vn_s, vn_r, rl_s, rl_r, nx_s, nx_r, ns_s, ns_r,
+    sbuf, rbuf, nextvec, doubled, fwd, bwd, acc, nx_part, nx_got, ns_out, ns_got, xp, xr,
+    load_sem, out_sem, a2a_s, a2a_r, x_s, x_r, g_s, g_r, vn_s, vn_r, rl_s, rl_r, nx_s, nx_r, ns_s, ns_r,
 ):
     slab, rep = lax.axis_index("clus"), lax.axis_index("rep")
     after = jnp.where(slab == SLABS - 1, 0, slab + 1)
@@ -79,7 +79,7 @@
         pltpu.make_async_copy(near_in.at[n], near.at[:, pl.ds(n * SIZE, SIZE)], load_sem.at[5 + n])
         for n in range(PAIRS)
     ]
-    for load in loads:
+    for load in loads[:3]:
         load.start()
 
     greeting = pltpu.get_barrier_semaphore()
@@ -93,6 +93,9 @@
                 greet(peer)
     for peer in rep_peers:
         pl.semaphore_signal(greeting, inc=1, device_id=(slab, peer), device_id_type=MESH)
+
+    for load in loads[3:]:
+        load.start()
 
     lane = lax.broadcasted_iota(jnp.int32, (16, COLS), 1)
     low = (lane < HALF).astype(F32).astype(BF16)
@@ -114,7 +117,7 @@
         vec[0, 0, :, :, pl.ds(pair * COLS, COLS)] = merged(even, swap_halves(odd)).reshape(part)
         vec[0, 1, :, :, pl.ds(pair * COLS, COLS)] = merged(swap_halves(even), odd).reshape(part)
 
-    def coefficients(m, g, first=0, last=STAGES):
+    def coefficients(m, g):
         values = vec[m, g].reshape(SIZE, WIDE)
 
         def multiply(ends):
@@ -151,9 +154,8 @@
                     send(stage, k, e, end)
             return 0
 
-        lax.fori_loop(first, last, step, 0)
-        if first == 0:
-            rbuf[m, g, slab] = sbuf[m, g, slab]
+        lax.fori_loop(0, STAGES, step, 0)
+        rbuf[m, g, slab] = sbuf[m, g, slab]
 
     def sent(m, g):
         others = pl.ds(0, SLABS - 1)
@@ -202,7 +204,16 @@
     def exchanges(m, g):
         return [
             pltpu.make_async_remote_copy(
-                xr.at[m, g, rep], xr.at[m, g, rep], x_s.at[m, g, k], x_r.at[m, g, k],
+                xp.at[m, g, peer], xr.at[m, g, rep], x_s.at[m, g, k], x_r.at[m, g, k],
+                device_id=(slab, peer), device_id_type=MESH,
+            )
+            for k, peer in enumerate(rep_peers)
+        ]
+
+    def gathers(m, g):
+        return [
+            pltpu.make_async_remote_copy(
+                vec.at[m + 1, g, rep], vec.at[m + 1, g, rep], g_s.at[m, g, k], g_r.at[m, g, k],
                 device_id=(slab, peer), device_id_type=MESH,
             )
             for k, peer in enumerate(rep_peers)
@@ -279,20 +290,32 @@
 
         step(0, 0)
         lax.fori_loop(1, STAGES, step, 0)
+
+    def exchange(m, g):
         next_sum(m, g).wait_recv()
         mine = pl.ds(pl.multiple_of(rep * QUARTER, QUARTER), QUARTER)
         acc[m, g, mine, :] += ns_got[m, g].astype(F32)
-        xr[m, g, rep] = acc[m, g].astype(BF16)
+        xp[m, g] = acc[m, g].astype(BF16).reshape(REPS, QUARTER, WIDE)
+        xr[m, g, rep] = xp[m, g, rep]
         for copy in exchanges(m, g):
             copy.start()
 
-    def image(m, g):
+    def reduce(m, g):
         for copy in exchanges(m, g):
             copy.wait_recv()
-        total = self_wide[...] * vec[m, g].reshape(SIZE, WIDE).astype(F32)
+        mine = pl.ds(pl.multiple_of(rep * QUARTER, QUARTER), QUARTER)
+        total = self_wide[mine, :] * vec[m, g, rep].astype(F32)
         for s in range(REPS):
             total += xr[m, g, s].astype(F32)
-        vec[m + 1, g] = total.astype(BF16).reshape(REPS, QUARTER, WIDE)
+        vec[m + 1, g, rep] = total.astype(BF16)
+        for copy in gathers(m, g):
+            copy.start()
+        if m == 0:
+            next_vector(1, g).start()
+
+    def image(m, g):
+        for copy in gathers(m, g):
+            copy.wait_recv()
 
     def write(m, out):
         return pltpu.make_async_copy(vec.at[m + 1], out, out_sem.at[m])
@@ -336,26 +359,32 @@
     self_wide[...] = jnp.concatenate(wide, axis=0).T
 
     far_terms(0, 0)
+    exchange(0, 0)
+    forward(0, 1)
+    reduce(0, 0)
     image(0, 0)
-    next_vector(1, 0).start()
     coefficients(1, 0)
-    forward(0, 1)
     far_terms(0, 1)
+    exchange(0, 1)
     backward(1, 0)
     pass_on(1, 0)
+    reduce(0, 1)
     sum_next(1, 0)
     image(0, 1)
-    next_vector(1, 1).start()
     coefficients(1, 1)
     forward(1, 0)
     backward(1, 1)
     far_terms(1, 0)
+    exchange(1, 0)
     pass_on(1, 1)
     sum_next(1, 1)
+    reduce(1, 0)
     write(0, first).start()
     forward(1, 1)
+    far_terms(1, 1)
+    exchange(1, 1)
     image(1, 0)
-    far_terms(1, 1)
+    reduce(1, 1)
     image(1, 1)
     write(1, second).start()
 
@@ -364,7 +393,7 @@
             sent(m, g).wait_send()
             next_vector(m, g).wait_send()
             next_sum(m, g).wait_send()
-            for copy in relays(m, g) + next_parts(m, g) + exchanges(m, g):
+            for copy in relays(m, g) + next_parts(m, g) + exchanges(m, g) + gathers(m, g):
                 copy.wait_send()
     write(0, first).wait()
     write(1, second).wait()
@@ -414,10 +443,12 @@
         vmem(both + (REPS, QUARTER, WIDE), BF16),
         vmem(both + (QUARTER, WIDE), BF16),
         vmem(both + (QUARTER, WIDE), BF16),
-        vmem(both + (REPS, SIZE, WIDE), BF16),
+        vmem(both + (REPS, QUARTER, WIDE), BF16),
+        vmem(both + (REPS, QUARTER, WIDE), BF16),
         dma((5 + PAIRS,)),
         dma((2,)),
         dma(both), dma(both + (STAGES,)),
+        dma(both + (3,)), dma(both + (3,)),
         dma(both + (3,)), dma(both + (3,)),
         dma(both), dma(both),
         dma(both + (3,)), dma(both + (3,)),

time: 91 us -> 88.4 us (0.971)
  the two profiles are of different devices: /device:TPU:64 before, /device:TPU:8 now
where the time goes in v3:
time: 88.4 us; the launch traced here: 88.2 us
  Pallas kernels  87.6 us (99%)
    pallas_call x1, Pallas kernels, local(): pl.pallas_call(kernel, out_shape=(grouped, grouped), in_specs=[hbm] * 6,...  85.6 us
    pallas_call x1, Pallas kernels, local(): pl.pallas_call(lay_out, out_shape=(image, image), in_specs=[whole, whole]...  1.96 us

profile of v3, /device:TPU:8, one launch (start us, length us, event | category | flops | bytes accessed | tf_op | source)
XLA Modules:
  0.0 88.2 jit_solution(13281856238786151073)
XLA Ops:
  0.6 85.6 %two_products.1 = (bf16[2,4,64,256]{3,2,1,0:T(8,128)(2,1)}, bf16[2,4,64,256]{3,2,1,0:T(8,128)(2,1)}) custom-call(s32[2,8]{1,0:T(2,128)} %bitcast.6, s32[128]{0:T(128)} %bitcast.7, bf16[1024,128]{1,0:T(8,128)(2,1)} %start_in.1, f32[8,128]{1,0:T(8,128)} %bitcast.5, bf16[8,256,256]{2,1,0:T(8,128)(2,1)} %near_in.1, bf16[128,32,256]{2,1,0:T(8,128)(2,1)} %bitcast.4), custom_call_target="tpu_custom_call" | custom-call | tf_op jit(solution)/shard_map/two_products/pallas_call | solution.py:460
  86.2 2.0 %lay_out.1 = (bf16[1024,128]{1,0:T(8,128)(2,1)}, bf16[1024,128]{1,0:T(8,128)(2,1)}) custom-call(bf16[2,4,64,256]{3,2,1,0:T(8,128)(2,1)} %get-tuple-element.4.first, bf16[2,4,64,256]{3,2,1,0:T(8,128)(2,1)} %get-tuple-element.5.second), custom_call_target="tpu_custom_call" | custom-call | tf_op jit(solution)/shard_map/lay_out/pallas_call | solution.py:471
